TPU v7x, 32 devices: a whole 2x2x4 slice. The times are simulated.
32 devices in a mesh: dp: 4 (over x, core), tensor: 8 (over z, y).
Axes of the slice: x: 2, y: 2, z: 4, core: 2. Of those that a mesh axis runs over, the one named last changes fastest.
Arguments:
- activations: bfloat16 [512, 29696], P('dp', 'tensor'), may hold values from -6 to 6
- weight_codes: bfloat16 [29696, 7424], P('tensor'), may hold values from -127 to 127, as said below
- channel_scale: float32 [7424], replicated, may hold values from 0.0006565322 to 0.0065653217
- output_grads: bfloat16 [512, 7424], P('dp', 'tensor'), may hold values from -0.375 to 0.375
Outputs:
- input_grads: float32 [512, 29696], P('dp', 'tensor')
- weight_grads: float32 [29696, 7424], P('tensor', 'dp')
Inputs may be any that keep to these rules, and one draw needn't show every extreme that they name: weight_codes holds whole numbers.
All inputs are finite; a program needn't handle non-finite values.
Results may differ from a plain program's by a relative error of at most 0.0029.
Values may be sent and summed in bfloat16 or wider, within the bound.
A program may use at most 128 MiB of HBM per device.

v0:
```python
import jax
import jax.numpy as jnp
from jax import lax
from jax.sharding import PartitionSpec as P


def per_device(activations, weight_codes, channel_scale, output_grads):
    full_rows = lax.all_gather(output_grads, "tensor", axis=1, tiled=True)
    scaled = (full_rows.astype(jnp.float32) * channel_scale).astype(jnp.bfloat16)
    input_grads = lax.dot_general(
        scaled, weight_codes, (((1,), (1,)), ((), ())), preferred_element_type=jnp.float32
    )
    grad_columns = lax.all_to_all(full_rows, "dp", split_axis=1, concat_axis=0, tiled=True)
    weight_grads = lax.dot_general(
        lax.all_gather(activations, "dp", axis=0, tiled=True),
        grad_columns,
        (((0,), (0,)), ((), ())),
        preferred_element_type=jnp.float32,
    )
    return (input_grads, weight_grads)


def solution(mesh):
    placed = (P("dp", "tensor"), P("tensor", None), P(), P("dp", "tensor"))
    return jax.shard_map(
        per_device,
        mesh=mesh,
        in_specs=placed,
        out_specs=(P("dp", "tensor"), P("tensor", "dp")),
        check_vma=False,
    )
```

profile of v0, /device:TPU:0, one launch (start us, length us, event | category | flops | bytes accessed | tf_op | source)
XLA Modules:
  0.0 131.5 jit_solution(15548972211753525182)
XLA Ops:
  7.2 0.0 copy-start.1
  7.2 0.0 all-gather.3.cloned.1.call-start
  7.2 0.7 all-gather.3.cloned.1.call-update
  7.9 0.0 all-gather.5.cloned.1.call-start
  8.0 0.7 all-gather.5.cloned.1.call-update
  8.7 51.1 %all-gather.3.cloned.1.call-done = bf16[128,7424]{0,1:T(8,128)(2,1)} async-done(((bf16[128,928]{0,1:T(8,128)(2,1)}), bf16[128,7424]{0,1:T(8,128)(2,1)}) %all-gather.3.cloned.1.call-update) | async-done | bytes 1900560 | tf_op jit(solution)/shard_map/all_gather | solution.py:8
  59.8 0.0 copy-start
  59.8 4.5 %all-to-all-start = ((bf16[128,4,1856]{0,2,1:T(8,128)(2,1)}), bf16[128,4,1856]{0,2,1:T(8,128)(2,1)}, u32[]{:S(2)}, u32[]{:S(2)}) async-start(bf16[128,4,1856]{0,2,1:T(8,128)(2,1)} %bitcast.6), calls=%async_computation | async-start | bytes 3801088 | tf_op jit(solution)/shard_map/all_to_all | solution.py:13
  64.3 0.0 copy-done.1
  64.3 0.0 copy-done
  64.4 27.5 %fusion = f32[128,3712]{1,0:T(8,128)} fusion(bf16[3712,7424]{1,0:T(8,128)(2,1)} %param.5, bf16[128,7424]{0,1:T(8,128)(2,1)S(1)} %copy-done, f32[7424]{0:T(1024)S(1)} %copy-done.1), kind=kOutput, calls=%fused_computation.1 | convolution fusion | flops 7057670144 | bytes 58946560 | tf_op jit(solution)/shard_map/dot_general | solution.py:10
  91.8 13.6 %all-to-all-done = bf16[128,4,1856]{0,2,1:T(8,128)(2,1)} async-done(((bf16[128,4,1856]{0,2,1:T(8,128)(2,1)}), bf16[128,4,1856]{0,2,1:T(8,128)(2,1)}, u32[]{:S(2)}, u32[]{:S(2)}) %all-to-all-start) | async-done | bytes 1900576 | tf_op jit(solution)/shard_map/all_to_all | solution.py:13
  105.5 2.8 %copy.7 = bf16[4,128,1856]{2,1,0:T(8,128)(2,1)S(1)} copy(bf16[4,128,1856]{1,2,0:T(8,128)(2,1)} %bitcast.1) | data formatting | bytes 3801088 | tf_op jit(solution)/shard_map/all_to_all | solution.py:13
  108.2 1.6 %all-gather.5.cloned.1.call-done = bf16[512,3712]{1,0:T(8,128)(2,1)} async-done(((bf16[128,3712]{1,0:T(8,128)(2,1)}), bf16[512,3712]{1,0:T(8,128)(2,1)}) %all-gather.5.cloned.1.call-update) | async-done | bytes 3801104 | tf_op jit(solution)/shard_map/all_gather | solution.py:15
  109.8 14.8 %fusion.2 = f32[3712,1856]{0,1:T(8,128)} fusion(bf16[512,3712]{1,0:T(8,128)(2,1)} %all-gather.5.cloned.1.call-done, bf16[512,1856]{1,0:T(8,128)(2,1)S(1)} %bitcast.7), kind=kOutput, calls=%fused_computation.3 | convolution fusion | flops 7054819328 | bytes 33259520 | tf_op jit(solution)/shard_map/dot_general | solution.py:14
Async XLA Ops:
  7.2 57.2 %copy-start.1 = (f32[7424]{0:T(1024)S(1)}, f32[7424]{0:T(1024)}, u32[]{:S(2)}) copy-start(f32[7424]{0:T(1024)} %param.6) | copy-start | bytes 89092
  7.2 52.6 %all-gather.3.cloned.1.call-start = ((), (), s32[]{:S(2)}) async-start(), calls=%async_computation.1 | async-start | bytes 2138112 | tf_op jit(solution)/shard_map/all_gather | solution.py:8
  7.9 101.9 %all-gather.5.cloned.1.call-start = ((), (), s32[]{:S(2)}) async-start(), calls=%async_computation.2 | async-start | bytes 4751360 | tf_op jit(solution)/shard_map/all_gather | solution.py:15
  59.8 4.6 %copy-start = (bf16[128,7424]{0,1:T(8,128)(2,1)S(1)}, bf16[128,7424]{0,1:T(8,128)(2,1)}, u32[]{:S(2)}) copy-start(bf16[128,7424]{0,1:T(8,128)(2,1)} %all-gather.3.cloned.1.call-done) | copy-start | bytes 5701636
  59.8 45.7 %all-to-all-start = ((bf16[128,4,1856]{0,2,1:T(8,128)(2,1)}), bf16[128,4,1856]{0,2,1:T(8,128)(2,1)}, u32[]{:S(2)}, u32[]{:S(2)}) async-start(bf16[128,4,1856]{0,2,1:T(8,128)(2,1)} %bitcast.6), calls=%async_computation | async-start | bytes 3801088 | tf_op jit(solution)/shard_map/all_to_all | solution.py:13
Sparse Core Ops, SparseCore 0:
  10.2 49.5 all-gather.2
  61.3 48.4 all-gather.4
where the time goes:
time: 132 us; the launch traced here: 131 us
  waiting for transfers between devices  67.7 us (51%)
  matrix products  42.3 us (32%)
  between operations  14.1 us (11%)
  starting transfers between devices  4.61 us (3%)
  local copies, waits for them, and re-layouts  2.78 us (2%)
    all_gather x1, waiting for transfers between devices, per_device(): full_rows = lax.all_gather(output_grads, 'tensor', axis=1, tiled=True)  51.1 us
    dot_general x1, matrix products, per_device(): lax.dot_general(scaled, weight_codes, (((1,), (1,)), ((), ())), preferred...  27.5 us
    dot_general x1, matrix products, per_device(): lax.dot_general(lax.all_gather(activations, 'dp', axis=0, tiled=True), gr...  14.8 us
    all_to_all x1, waiting for transfers between devices, per_device(): lax.all_to_all(full_rows, 'dp', split_axis=1, concat_axis=0, tiled=True)  13.6 us
    all_to_all x1, starting transfers between devices, per_device(): lax.all_to_all(full_rows, 'dp', split_axis=1, concat_axis=0, tiled=True)  4.54 us
    all_to_all x1, local copies, waits for them, and re-layouts, per_device(): lax.all_to_all(full_rows, 'dp', split_axis=1, concat_axis=0, tiled=True)  2.77 us
  transfers between devices with their start and end apart: 3, of which 3 were waited for; matrix products, arithmetic and copies ran while one was open for 23% of the time, Pallas kernels for 0%

commit v1 on v0

v1 whole, which is shorter than its diff:
```python
import functools

import jax
import jax.numpy as jnp
from jax import lax
from jax.experimental import pallas as pl
from jax.experimental.pallas import tpu as pltpu
from jax.sharding import PartitionSpec as P

MESH = pl.DeviceIdType.MESH
BF16, F32 = jnp.bfloat16, jnp.float32
LINE = 4
LANES = 128


def gather_kernel(
    a_ref, g_ref, s_ref, w_ref, ig_ref, at_ref, og_ref,
    codes, gbuf, cross, gs, scale, acc, ig_own, ig_sib,
    code_sem, up_sem, down_sem, y_sem, sib_sem, line_recv, y_recv, sib_recv,
    cross_sem, cup_sem, cdown_sem, cy_sem, cross_recv, cy_recv,
    ax_sem, as_sem, ax_recv, as_recv, al_sem, og_sem, ig_sem, g_sem,
):
    dp, j = lax.axis_index("dp"), lax.axis_index("tensor")
    x, c = lax.div(dp, 2), lax.rem(dp, 2)
    z, y = lax.div(j, 2), lax.rem(j, 2)
    hidden = a_ref.shape[1]
    channels = g_ref.shape[0]
    depth = w_ref.shape[1]
    rows = codes.shape[0]
    step_rows = hidden - rows
    half = depth // 2
    sibling = (2 * x + 1 - c, j)
    across = (2 * (1 - x) + c, j)
    beside = (dp, 2 * z + 1 - y)
    above = (dp, j + 2)
    below = (dp, j - 2)

    def code_copy(i):
        n = rows // 5
        return pltpu.make_async_copy(
            w_ref.at[pl.ds(pl.multiple_of(c * step_rows + i * n, 128), n)],
            codes.at[pl.ds(i * n, n)], code_sem.at[i])

    for i in range(5):
        code_copy(i).start()

    barrier = pltpu.get_barrier_semaphore()

    def greet(device):
        pl.semaphore_signal(barrier, inc=1, device_id=device, device_id_type=MESH)

    greet(sibling)
    greet(beside)
    greet((2 * (1 - x), j))
    greet((2 * (1 - x) + 1, j))

    @pl.when(z < LINE - 1)
    def _():
        greet(above)

    @pl.when(z > 0)
    def _():
        greet(below)

    g_local = pltpu.make_async_copy(
        g_ref, gbuf.at[c, pl.ds(pl.multiple_of(j * channels, 32), channels)], g_sem.at[0])
    g_local.start()

    ends = jnp.logical_or(z == 0, z == LINE - 1)
    pl.semaphore_wait(barrier, jnp.where(ends, 5, 6))

    def remote(src, dst, send, recv, device):
        return pltpu.make_async_remote_copy(
            src_ref=src, dst_ref=dst, send_sem=send, recv_sem=recv,
            device_id=device, device_id_type=MESH)

    def slot(core, zz, yy):
        start = pl.multiple_of((2 * zz + yy) * channels, 32)
        return gbuf.at[core, pl.ds(start, channels)]

    def up(zz, src=None):
        s = slot(c, zz, y)
        return remote(s if src is None else src, s, up_sem.at[zz], line_recv.at[zz], above)

    def down(zz, src=None):
        s = slot(c, zz, y)
        return remote(s if src is None else src, s, down_sem.at[zz], line_recv.at[zz], below)

    def side(zz, src=None):
        s = slot(c, zz, y)
        return remote(s if src is None else src, s, y_sem.at[zz], y_recv.at[zz], beside)

    def from_side(zz):
        s = slot(c, zz, 1 - y)
        return remote(s, s, y_sem.at[zz], y_recv.at[zz], beside)

    def to_sib(zz, yy, src=None):
        s = slot(c, zz, yy)
        k = 2 * zz + yy
        return remote(s if src is None else src, s, sib_sem.at[k], sib_recv.at[k], sibling)

    def from_sib(zz, yy):
        s = slot(1 - c, zz, yy)
        k = 2 * zz + yy
        return remote(s, s, sib_sem.at[k], sib_recv.at[k], sibling)

    entry = 2 * x + c
    away = jnp.abs(z - entry)
    sends_cross = lax.div(z, 2) != x

    def cross_out():
        return remote(g_ref, cross.at[c, y], cross_sem.at[0], cross_recv.at[c],
                      (2 * (1 - x) + lax.rem(z, 2), j))

    def cross_move(k, send, recv, device):
        return remote(cross.at[k, y], cross.at[k, y], send.at[k], recv.at[k], device)

    def cross_up(k):
        return cross_move(k, cup_sem, cross_recv, above)

    def cross_down(k):
        return cross_move(k, cdown_sem, cross_recv, below)

    def cross_side(k):
        return cross_move(k, cy_sem, cy_recv, beside)

    def cross_from_side(k):
        return remote(cross.at[k, 1 - y], cross.at[k, 1 - y], cy_sem.at[k], cy_recv.at[k], beside)

    goes_up = jnp.logical_and(z >= entry, z < LINE - 1)
    goes_down = jnp.logical_and(z <= entry, z > 0)

    @pl.when(sends_cross)
    def _():
        cross_out().start()

    @pl.when(z < LINE - 1)
    def _():
        up(z, g_ref).start()

    @pl.when(z > 0)
    def _():
        down(z, g_ref).start()

    side(z, g_ref).start()
    to_sib(z, y, g_ref).start()

    piece = a_ref.shape[0] // 4

    def acts(i, index):
        start = pl.multiple_of(index * a_ref.shape[0] + i * piece, piece)
        return at_ref.at[pl.ds(start, piece)]

    def own_acts(i):
        return a_ref.at[pl.ds(i * piece, piece)]

    def acts_across(i):
        return remote(own_acts(i), acts(i, dp), ax_sem.at[i], ax_recv.at[i], across)

    def acts_from_across(i):
        s = acts(i, 2 * (1 - x) + c)
        return remote(s, s, ax_sem.at[i], ax_recv.at[i], across)

    def acts_sib(i):
        return remote(own_acts(i), acts(i, dp), as_sem.at[i], as_recv.at[i], sibling)

    def acts_from_sib(i):
        s = acts(i, 2 * x + 1 - c)
        return remote(s, s, as_sem.at[i], as_recv.at[i], sibling)

    def acts_on(i):
        s = acts(i, 2 * (1 - x) + c)
        return remote(s, s, as_sem.at[4 + i], as_recv.at[4 + i], sibling)

    def acts_on_from(i):
        s = acts(i, 2 * (1 - x) + 1 - c)
        return remote(s, s, as_sem.at[4 + i], as_recv.at[4 + i], sibling)

    def acts_local(i):
        return pltpu.make_async_copy(own_acts(i), acts(i, dp), al_sem.at[i])

    for i in range(4):
        acts_across(i).start()
    for i in range(4):
        acts_sib(i).start()
        acts_local(i).start()

    @pl.loop(0, depth // LANES)
    def _(t):
        r = pl.ds(pl.multiple_of(t * LANES, LANES), LANES)
        scale[r, :] = jnp.broadcast_to(s_ref[r][None, :], (LANES, LANES)).T

    def relay_cross():
        for k in range(2):
            cross_up(k).wait_recv()

            @pl.when(goes_up)
            def _():
                cross_up(k).start()

            @pl.when(goes_down)
            def _():
                cross_down(k).start()

            cross_side(k).start()

    def pass_side(d):
        def one(zz):
            from_side(zz).wait_recv()
            to_sib(zz, 1 - y).start()

        if d == 0:
            one(z)
        else:
            pl.when(z - d >= 0)(lambda: one(z - d))
            pl.when(z + d <= LINE - 1)(lambda: one(z + d))

    for d in range(1, LINE):
        @pl.when(z - d >= 0)
        def _():
            zz = z - d
            up(zz).wait_recv()

            @pl.when(z < LINE - 1)
            def _():
                up(zz).start()

            side(zz).start()
            to_sib(zz, y).start()

        @pl.when(z + d <= LINE - 1)
        def _():
            zz = z + d
            down(zz).wait_recv()

            @pl.when(z > 0)
            def _():
                down(zz).start()

            side(zz).start()
            to_sib(zz, y).start()

        pl.when(away == d - 1)(relay_cross)
        if d >= 2:
            pass_side(d - 2)

    g_local.wait()
    for i in range(5):
        code_copy(i).wait()

    def multiply(h, first):
        for zz in range(2):
            for yy in range(2):
                from_sib(2 * h + zz, yy).wait_recv()
        base = h * half

        @pl.loop(0, half // LANES)
        def _(t):
            r = pl.ds(pl.multiple_of(base + t * LANES, LANES), LANES)
            q = pl.ds(pl.multiple_of(t * LANES, LANES), LANES)
            by = scale[r, :]
            gs[q, :LANES] = (gbuf[0, r, :].astype(F32) * by).astype(BF16)
            gs[q, LANES:] = (gbuf[1, r, :].astype(F32) * by).astype(BF16)

        tile = rows // 5

        @pl.loop(0, 5)
        def _(t):
            r = pl.ds(pl.multiple_of(t * tile, tile), tile)
            k = pl.ds(pl.multiple_of(base, LANES), half)
            part = jnp.dot(codes[r, k], gs[...], preferred_element_type=F32)
            acc[r, :] = part if first else acc[r, :] + part

    near = lax.div(z, 2)
    multiply(near, True)
    pl.when(away == LINE - 1)(relay_cross)
    pass_side(LINE - 2)
    pass_side(LINE - 1)
    for i in range(2):
        acts_from_across(i).wait_recv()
        acts_on(i).start()
    multiply(1 - near, False)

    @pl.loop(0, rows // LANES)
    def _(t):
        r = pl.ds(pl.multiple_of(t * LANES, LANES), LANES)
        ig_sib[:, r] = acc[r, pl.ds(pl.multiple_of((1 - c) * LANES, LANES), LANES)].T
        ig_own[:, r] = acc[r, pl.ds(pl.multiple_of(c * LANES, LANES), LANES)].T

    def ig_out():
        return remote(
            ig_sib.at[:, pl.ds(pl.multiple_of(c * (rows - step_rows), LANES), step_rows)],
            ig_ref.at[:, pl.ds(pl.multiple_of(c * rows, LANES), step_rows)],
            ig_sem.at[0], ig_sem.at[1], sibling)

    def ig_in():
        s = ig_ref.at[:, pl.ds(pl.multiple_of((1 - c) * rows, LANES), step_rows)]
        return remote(s, s, ig_sem.at[0], ig_sem.at[1], sibling)

    ig_local = pltpu.make_async_copy(
        ig_own, ig_ref.at[:, pl.ds(pl.multiple_of(c * step_rows, LANES), rows)], ig_sem.at[2])
    ig_out().start()
    ig_local.start()

    for i in range(2, 4):
        acts_from_across(i).wait_recv()
        acts_on(i).start()

    block = pl.ds(pl.multiple_of(2 * entry * channels, 32), 2 * channels)
    og_copies = [
        pltpu.make_async_copy(gbuf.at[k, block], og_ref.at[2 * x + k], og_sem.at[k])
        for k in range(2)
    ]
    for k in range(2):
        og_copies[k].start()
    for k in range(2):
        cross_from_side(k).wait_recv()
        for yy in range(2):
            og_copies.append(pltpu.make_async_copy(
                cross.at[k, yy], og_ref.at[2 * (1 - x) + k, pl.ds(yy * channels, channels)],
                og_sem.at[2 + 2 * k + yy]))
            og_copies[-1].start()

    for zz in range(LINE):
        @pl.when(jnp.logical_and(zz <= z, z < LINE - 1))
        def _():
            up(zz).wait_send()

        @pl.when(jnp.logical_and(zz >= z, z > 0))
        def _():
            down(zz).wait_send()

        side(zz).wait_send()
        for yy in range(2):
            to_sib(zz, yy).wait_send()

    @pl.when(sends_cross)
    def _():
        cross_out().wait_send()

    for k in range(2):
        @pl.when(goes_up)
        def _():
            cross_up(k).wait_send()

        @pl.when(goes_down)
        def _():
            cross_down(k).wait_send()

        cross_side(k).wait_send()

    for i in range(4):
        acts_across(i).wait_send()
        acts_sib(i).wait_send()
        acts_on(i).wait_send()
        acts_local(i).wait()
        acts_from_sib(i).wait_recv()
        acts_on_from(i).wait_recv()
    for copy in og_copies:
        copy.wait()
    ig_local.wait()
    ig_out().wait_send()
    ig_in().wait_recv()


def weight_kernel(o_ref, a_ref, out_ref):
    o = jnp.concatenate([o_ref[k] for k in range(4)], axis=1)
    out_ref[...] = jnp.dot(o, a_ref[...], preferred_element_type=F32)


def per_device_kernels(activations, weight_codes, channel_scale, output_grads):
    tokens, hidden = activations.shape
    channels = output_grads.shape[1]
    depth = weight_codes.shape[1]
    rows = (hidden // LANES + 1) // 2 * LANES
    dma = pltpu.SemaphoreType.DMA
    vmem = pl.BlockSpec(memory_space=pltpu.VMEM)
    anywhere = pl.BlockSpec(memory_space=pl.ANY)
    input_grads, acts, grads = pl.pallas_call(
        gather_kernel,
        out_shape=(
            jax.ShapeDtypeStruct((tokens, hidden), F32),
            jax.ShapeDtypeStruct((4 * tokens, hidden), BF16),
            jax.ShapeDtypeStruct((4, 2 * channels, tokens), BF16),
        ),
        in_specs=[anywhere, anywhere, vmem, anywhere],
        out_specs=(anywhere,) * 3,
        scratch_shapes=[
            pltpu.VMEM((rows, depth), BF16),
            pltpu.VMEM((2, depth, tokens), BF16),
            pltpu.VMEM((2, 2, channels, tokens), BF16),
            pltpu.VMEM((depth // 2, 2 * tokens), BF16),
            pltpu.VMEM((depth, LANES), F32),
            pltpu.VMEM((rows, 2 * tokens), F32),
            pltpu.VMEM((tokens, rows), F32),
            pltpu.VMEM((tokens, rows), F32),
            dma((5,)), dma((4,)), dma((4,)), dma((4,)), dma((8,)), dma((4,)), dma((4,)), dma((8,)),
            dma((1,)), dma((2,)), dma((2,)), dma((2,)), dma((2,)), dma((2,)),
            dma((4,)), dma((8,)), dma((4,)), dma((8,)), dma((4,)), dma((6,)), dma((3,)), dma((1,)),
        ],
        compiler_params=pltpu.CompilerParams(
            collective_id=0, has_side_effects=True, vmem_limit_bytes=56 * 2**20),
    )(activations, output_grads.T, channel_scale, weight_codes)
    tile = 256
    weight_grads = pl.pallas_call(
        weight_kernel,
        grid=(pl.cdiv(2 * channels, tile),),
        out_shape=jax.ShapeDtypeStruct((2 * channels, hidden), F32),
        in_specs=[
            pl.BlockSpec((4, tile, tokens), lambda i: (0, i, 0)),
            pl.BlockSpec((4 * tokens, hidden), lambda i: (0, 0)),
        ],
        out_specs=pl.BlockSpec((tile, hidden), lambda i: (i, 0)),
        compiler_params=pltpu.CompilerParams(vmem_limit_bytes=40 * 2**20),
    )(grads, acts)
    return input_grads, weight_grads.T


def per_device_plain(activations, weight_codes, channel_scale, output_grads):
    full_rows = lax.all_gather(output_grads, "tensor", axis=1, tiled=True)
    scaled = (full_rows.astype(F32) * channel_scale).astype(BF16)
    input_grads = lax.dot_general(
        scaled, weight_codes, (((1,), (1,)), ((), ())), preferred_element_type=F32)
    grad_columns = lax.all_to_all(full_rows, "dp", split_axis=1, concat_axis=0, tiled=True)
    weight_grads = lax.dot_general(
        lax.all_gather(activations, "dp", axis=0, tiled=True), grad_columns,
        (((0,), (0,)), ((), ())), preferred_element_type=F32)
    return input_grads, weight_grads


def solution(mesh):
    placed = (P("dp", "tensor"), P("tensor", None), P(), P("dp", "tensor"))
    small = mesh.shape["dp"] == 4 and mesh.shape["tensor"] == 2 * LINE

    return jax.shard_map(
        per_device_kernels if small else per_device_plain,
        mesh=mesh,
        in_specs=placed,
        out_specs=(P("dp", "tensor"), P("tensor", "dp")),
        check_vma=False,
    )
```

time: 132 us -> 71.9 us (0.54)
  the two profiles are of different devices: /device:TPU:0 before, /device:TPU:7 now
where the time goes in v1:
time: 71.9 us; the launch traced here: 71.6 us
  Pallas kernels  66.1 us (92%)
  local copies, waits for them, and re-layouts  4.84 us (7%)
    pallas_call x1, Pallas kernels, per_device_kernels(): pl.pallas_call(gather_kernel, out_shape=(jax.ShapeDtypeStruct((tokens, hi...  53.3 us
    pallas_call x1, Pallas kernels, per_device_kernels(): pl.pallas_call(weight_kernel, grid=(pl.cdiv(2 * channels, tile),), out_sh...  12.8 us
    unnamed x7, local copies, waits for them, and re-layouts  4.84 us

profile of v1, /device:TPU:7, one launch (start us, length us, event | category | flops | bytes accessed | tf_op | source)
XLA Modules:
  0.0 71.6 jit_solution(8612518550100182073)
XLA Ops:
  0.6 53.3 %shard_map.59 = (f32[128,3712]{1,0:T(8,128)}, bf16[512,3712]{1,0:T(8,128)(2,1)}, bf16[4,1856,128]{2,1,0:T(8,128)(2,1)}) custom-call(bf16[128,3712]{1,0:T(8,128)(2,1)} %a_ref.1, bf16[928,128]{1,0:T(8,128)(2,1)} %bitcast.3, f32[7424]{0:T(1024)} %s_ref.1, bf16[3712,7424]{1,0:T(8,128)(2,1)} %w_ref.1), custom_call_target="tpu_custom_call" | custom-call | tf_op jit(solution)/shard_map/pallas_call | solution.py:379
  53.9 0.0 copy-start
  53.9 2.1 %copy-done = bf16[512,3712]{1,0:T(8,128)(2,1)S(1)} copy-done((bf16[512,3712]{1,0:T(8,128)(2,1)S(1)}, bf16[512,3712]{1,0:T(8,128)(2,1)}, u32[]{:S(2)}) %copy-start) | copy-done | bytes 3801112
  56.0 0.0 copy-start.1
  56.0 1.5 %copy-done.1 = bf16[4,1856,128]{2,1,0:T(8,128)(2,1)S(1)} copy-done((bf16[4,1856,128]{2,1,0:T(8,128)(2,1)S(1)}, bf16[4,1856,128]{2,1,0:T(8,128)(2,1)}, u32[]{:S(2)}) %copy-start.1) | copy-done | bytes 1900568
  57.5 0.0 copy-start.2
  57.5 12.8 %shard_map.60 = f32[1856,3712]{1,0:T(8,128)} custom-call(bf16[4,1856,128]{2,1,0:T(8,128)(2,1)S(1)} %copy-done.1, bf16[512,3712]{1,0:T(8,128)(2,1)S(1)} %copy-done), custom_call_target="tpu_custom_call" | custom-call | tf_op jit(solution)/shard_map/pallas_call | solution.py:405
  70.4 0.0 copy-done.2
  70.4 1.2 %copy.7 = f32[128,3712]{1,0:T(8,128)} copy(f32[128,3712]{1,0:T(8,128)S(1)} %copy-done.2) | data formatting | bytes 3801088
Async XLA Ops:
  53.9 2.1 %copy-start = (bf16[512,3712]{1,0:T(8,128)(2,1)S(1)}, bf16[512,3712]{1,0:T(8,128)(2,1)}, u32[]{:S(2)}) copy-start(bf16[512,3712]{1,0:T(8,128)(2,1)} %get-tuple-element.7.a_ref) | copy-start | bytes 11403268
  56.0 1.5 %copy-start.1 = (bf16[4,1856,128]{2,1,0:T(8,128)(2,1)S(1)}, bf16[4,1856,128]{2,1,0:T(8,128)(2,1)}, u32[]{:S(2)}) copy-start(bf16[4,1856,128]{2,1,0:T(8,128)(2,1)} %get-tuple-element.6.o_ref) | copy-start | bytes 5701636
  57.5 12.9 %copy-start.2 = (f32[128,3712]{1,0:T(8,128)S(1)}, f32[128,3712]{1,0:T(8,128)}, u32[]{:S(2)}) copy-start(f32[128,3712]{1,0:T(8,128)} %get-tuple-element.10) | copy-start | bytes 5701636

commit v2 on v1

--- a/solution.py
+++ b/solution.py
@@ -15,7 +15,7 @@
 
 def gather_kernel(
     a_ref, g_ref, s_ref, w_ref, ig_ref, at_ref, og_ref,
-    codes, gbuf, cross, gs, scale, acc, ig_own, ig_sib,
+    codes, gbuf, cross, gs, acc,
     code_sem, up_sem, down_sem, y_sem, sib_sem, line_recv, y_recv, sib_recv,
     cross_sem, cup_sem, cdown_sem, cy_sem, cross_recv, cy_recv,
     ax_sem, as_sem, ax_recv, as_recv, al_sem, og_sem, ig_sem, g_sem,
@@ -185,11 +185,6 @@
         acts_sib(i).start()
         acts_local(i).start()
 
-    @pl.loop(0, depth // LANES)
-    def _(t):
-        r = pl.ds(pl.multiple_of(t * LANES, LANES), LANES)
-        scale[r, :] = jnp.broadcast_to(s_ref[r][None, :], (LANES, LANES)).T
-
     def relay_cross():
         for k in range(2):
             cross_up(k).wait_recv()
@@ -258,9 +253,9 @@
         def _(t):
             r = pl.ds(pl.multiple_of(base + t * LANES, LANES), LANES)
             q = pl.ds(pl.multiple_of(t * LANES, LANES), LANES)
-            by = scale[r, :]
-            gs[q, :LANES] = (gbuf[0, r, :].astype(F32) * by).astype(BF16)
-            gs[q, LANES:] = (gbuf[1, r, :].astype(F32) * by).astype(BF16)
+            by = s_ref[r][None, :]
+            gs[:LANES, q] = (gbuf[0, r, :].astype(F32).T * by).astype(BF16)
+            gs[LANES:, q] = (gbuf[1, r, :].astype(F32).T * by).astype(BF16)
 
         tile = rows // 5
 
@@ -268,8 +263,9 @@
         def _(t):
             r = pl.ds(pl.multiple_of(t * tile, tile), tile)
             k = pl.ds(pl.multiple_of(base, LANES), half)
-            part = jnp.dot(codes[r, k], gs[...], preferred_element_type=F32)
-            acc[r, :] = part if first else acc[r, :] + part
+            part = lax.dot_general(
+                gs[...], codes[r, k], (((1,), (1,)), ((), ())), preferred_element_type=F32)
+            acc[:, r] = part if first else acc[:, r] + part
 
     near = lax.div(z, 2)
     multiply(near, True)
@@ -281,15 +277,12 @@
         acts_on(i).start()
     multiply(1 - near, False)
 
-    @pl.loop(0, rows // LANES)
-    def _(t):
-        r = pl.ds(pl.multiple_of(t * LANES, LANES), LANES)
-        ig_sib[:, r] = acc[r, pl.ds(pl.multiple_of((1 - c) * LANES, LANES), LANES)].T
-        ig_own[:, r] = acc[r, pl.ds(pl.multiple_of(c * LANES, LANES), LANES)].T
+    def tokens_of(core):
+        return pl.ds(pl.multiple_of(core * LANES, LANES), LANES)
 
     def ig_out():
         return remote(
-            ig_sib.at[:, pl.ds(pl.multiple_of(c * (rows - step_rows), LANES), step_rows)],
+            acc.at[tokens_of(1 - c), pl.ds(pl.multiple_of(c * (rows - step_rows), LANES), step_rows)],
             ig_ref.at[:, pl.ds(pl.multiple_of(c * rows, LANES), step_rows)],
             ig_sem.at[0], ig_sem.at[1], sibling)
 
@@ -298,7 +291,7 @@
         return remote(s, s, ig_sem.at[0], ig_sem.at[1], sibling)
 
     ig_local = pltpu.make_async_copy(
-        ig_own, ig_ref.at[:, pl.ds(pl.multiple_of(c * step_rows, LANES), rows)], ig_sem.at[2])
+        acc.at[tokens_of(c)], ig_ref.at[:, pl.ds(pl.multiple_of(c * step_rows, LANES), rows)], ig_sem.at[2])
     ig_out().start()
     ig_local.start()
 
@@ -363,9 +356,66 @@
     ig_in().wait_recv()
 
 
-def weight_kernel(o_ref, a_ref, out_ref):
-    o = jnp.concatenate([o_ref[k] for k in range(4)], axis=1)
-    out_ref[...] = jnp.dot(o, a_ref[...], preferred_element_type=F32)
+TILE = 256
+PARTS = 4
+
+
+def weight_kernel(o_ref, a_ref, ig_ref, out_ref, ig_out, o, a, out, o_sem, a_sem, ig_sem, out_sem):
+    channels = out_ref.shape[0]
+    tokens = a_ref.shape[0] // 4
+    loads = [pltpu.make_async_copy(o_ref.at[k], o.at[k], o_sem.at[k]) for k in range(4)]
+    for k in range(4):
+        rows = pl.ds(k * tokens, tokens)
+        loads.append(pltpu.make_async_copy(a_ref.at[rows], a.at[rows], a_sem.at[k]))
+    ig_copy = pltpu.make_async_copy(ig_ref, ig_out, ig_sem.at[0])
+    for load in loads:
+        load.start()
+    ig_copy.start()
+    for load in loads:
+        load.wait()
+
+    full = channels // TILE
+    rest = channels % TILE
+    n = TILE // PARTS
+
+    def write(slot, t, i):
+        start = pl.multiple_of(t * TILE + i * n, n)
+        return pltpu.make_async_copy(
+            out.at[slot, pl.ds(i * n, n)], out_ref.at[pl.ds(start, n)], out_sem.at[slot, i])
+
+    def product(start, size):
+        rows = pl.ds(start, size)
+        left = jnp.concatenate([o[k, rows, :] for k in range(4)], axis=1)
+        return jnp.dot(left, a[...], preferred_element_type=F32)
+
+    @pl.loop(0, full)
+    def _(t):
+        slot = lax.rem(t, 3)
+
+        @pl.when(t >= 3)
+        def _():
+            for i in range(PARTS):
+                write(slot, t - 3, i).wait()
+
+        out[slot] = product(pl.multiple_of(t * TILE, TILE), TILE)
+        for i in range(PARTS):
+            write(slot, t, i).start()
+
+    last = full % 3
+    for i in range(PARTS):
+        write(last, full - 3, i).wait()
+    out[last, :rest] = product(full * TILE, rest)
+    ends = []
+    for i in range(rest // n):
+        ends.append(write(last, full, i))
+    for end in ends:
+        end.start()
+    for t in (full - 2, full - 1):
+        for i in range(PARTS):
+            write(t % 3, t, i).wait()
+    for end in ends:
+        end.wait()
+    ig_copy.wait()
 
 
 def per_device_kernels(activations, weight_codes, channel_scale, output_grads):
@@ -389,11 +439,8 @@
             pltpu.VMEM((rows, depth), BF16),
             pltpu.VMEM((2, depth, tokens), BF16),
             pltpu.VMEM((2, 2, channels, tokens), BF16),
-            pltpu.VMEM((depth // 2, 2 * tokens), BF16),
-            pltpu.VMEM((depth, LANES), F32),
-            pltpu.VMEM((rows, 2 * tokens), F32),
-            pltpu.VMEM((tokens, rows), F32),
-            pltpu.VMEM((tokens, rows), F32),
+            pltpu.VMEM((2 * tokens, depth // 2), BF16),
+            pltpu.VMEM((2 * tokens, rows), F32),
             dma((5,)), dma((4,)), dma((4,)), dma((4,)), dma((8,)), dma((4,)), dma((4,)), dma((8,)),
             dma((1,)), dma((2,)), dma((2,)), dma((2,)), dma((2,)), dma((2,)),
             dma((4,)), dma((8,)), dma((4,)), dma((8,)), dma((4,)), dma((6,)), dma((3,)), dma((1,)),
@@ -401,18 +448,22 @@
         compiler_params=pltpu.CompilerParams(
             collective_id=0, has_side_effects=True, vmem_limit_bytes=56 * 2**20),
     )(activations, output_grads.T, channel_scale, weight_codes)
-    tile = 256
-    weight_grads = pl.pallas_call(
+    weight_grads, input_grads = pl.pallas_call(
         weight_kernel,
-        grid=(pl.cdiv(2 * channels, tile),),
-        out_shape=jax.ShapeDtypeStruct((2 * channels, hidden), F32),
-        in_specs=[
-            pl.BlockSpec((4, tile, tokens), lambda i: (0, i, 0)),
-            pl.BlockSpec((4 * tokens, hidden), lambda i: (0, 0)),
+        out_shape=(
+            jax.ShapeDtypeStruct((2 * channels, hidden), F32),
+            jax.ShapeDtypeStruct((tokens, hidden), F32),
+        ),
+        in_specs=[anywhere] * 3,
+        out_specs=(anywhere,) * 2,
+        scratch_shapes=[
+            pltpu.VMEM((4, 2 * channels, tokens), BF16),
+            pltpu.VMEM((4 * tokens, hidden), BF16),
+            pltpu.VMEM((3, TILE, hidden), F32),
+            dma((4,)), dma((4,)), dma((1,)), dma((3, PARTS)),
         ],
-        out_specs=pl.BlockSpec((tile, hidden), lambda i: (i, 0)),
-        compiler_params=pltpu.CompilerParams(vmem_limit_bytes=40 * 2**20),
-    )(grads, acts)
+        compiler_params=pltpu.CompilerParams(vmem_limit_bytes=56 * 2**20),
+    )(grads, acts, input_grads)
     return input_grads, weight_grads.T
 
 

time: 71.9 us -> 119 us (1.66)
  Pallas kernels: 66.1 us -> 118 us
  local copies, waits for them, and re-layouts: 4.84 us -> 0 us
    pallas_call x1, Pallas kernels: 12.8 us -> 58.9 us  [per_device_kernels(): pl.pallas_call(weight_kernel, out_shape=(jax.ShapeDtypeStruct((2 * channe...]
    pallas_call x1, Pallas kernels: 53.3 us -> 59.1 us  [per_device_kernels(): pl.pallas_call(gather_kernel, out_shape=(jax.ShapeDtypeStruct((tokens, hi...]
    unnamed x7 -> x0, local copies, waits for them, and re-layouts: 4.84 us -> none
where the time goes in v2:
time: 119 us
  Pallas kernels  118 us (99%)
    pallas_call x1, Pallas kernels, per_device_kernels(): pl.pallas_call(gather_kernel, out_shape=(jax.ShapeDtypeStruct((tokens, hi...  59.1 us
    pallas_call x1, Pallas kernels, per_device_kernels(): pl.pallas_call(weight_kernel, out_shape=(jax.ShapeDtypeStruct((2 * channe...  58.9 us

profile of v2, /device:TPU:7, one launch (start us, length us, event | category | flops | bytes accessed | tf_op | source)
XLA Modules:
  0.0 118.7 jit_solution(2102274882699471860)
XLA Ops:
  0.6 59.1 %shard_map.59 = (f32[128,3712]{1,0:T(8,128)}, bf16[512,3712]{1,0:T(8,128)(2,1)}, bf16[4,1856,128]{2,1,0:T(8,128)(2,1)}) custom-call(bf16[128,3712]{1,0:T(8,128)(2,1)} %a_ref.1, bf16[928,128]{1,0:T(8,128)(2,1)} %bitcast.2, f32[7424]{0:T(1024)} %s_ref.1, bf16[3712,7424]{1,0:T(8,128)(2,1)} %w_ref.1), custom_call_target="tpu_custom_call" | custom-call | tf_op jit(solution)/shard_map/pallas_call | solution.py:429
  59.8 58.9 %shard_map.60 = (f32[1856,3712]{1,0:T(8,128)}, f32[128,3712]{1,0:T(8,128)}) custom-call(bf16[4,1856,128]{2,1,0:T(8,128)(2,1)} %get-tuple-element.7.o_ref, bf16[512,3712]{1,0:T(8,128)(2,1)} %get-tuple-element.8.a_ref, f32[128,3712]{1,0:T(8,128)} %get-tuple-element.9.ig_ref), custom_call_target="tpu_custom_call" | custom-call | tf_op jit(solution)/shard_map/pallas_call | solution.py:451

commit v3 on v2

--- a/solution.py
+++ b/solution.py
@@ -15,10 +15,10 @@
 
 def gather_kernel(
     a_ref, g_ref, s_ref, w_ref, ig_ref, at_ref, og_ref,
-    codes, gbuf, cross, gs, acc,
+    codes, gbuf, cross, gs, scale, acc, ig_own, ig_sib, held,
     code_sem, up_sem, down_sem, y_sem, sib_sem, line_recv, y_recv, sib_recv,
     cross_sem, cup_sem, cdown_sem, cy_sem, cross_recv, cy_recv,
-    ax_sem, as_sem, ax_recv, as_recv, al_sem, og_sem, ig_sem, g_sem,
+    ax_sem, as_sem, ax_recv, as_recv, al_sem, og_sem, ig_sem, g_sem, held_sem,
 ):
     dp, j = lax.axis_index("dp"), lax.axis_index("tensor")
     x, c = lax.div(dp, 2), lax.rem(dp, 2)
@@ -41,9 +41,8 @@
             w_ref.at[pl.ds(pl.multiple_of(c * step_rows + i * n, 128), n)],
             codes.at[pl.ds(i * n, n)], code_sem.at[i])
 
-    for i in range(5):
-        code_copy(i).start()
-
+    held_load = pltpu.make_async_copy(a_ref, held.at[0], held_sem.at[0])
+    held_load.start()
     barrier = pltpu.get_barrier_semaphore()
 
     def greet(device):
@@ -151,39 +150,50 @@
         start = pl.multiple_of(index * a_ref.shape[0] + i * piece, piece)
         return at_ref.at[pl.ds(start, piece)]
 
-    def own_acts(i):
-        return a_ref.at[pl.ds(i * piece, piece)]
+    def kept(k, i):
+        return held.at[k, pl.ds(i * piece, piece)]
 
     def acts_across(i):
-        return remote(own_acts(i), acts(i, dp), ax_sem.at[i], ax_recv.at[i], across)
-
-    def acts_from_across(i):
-        s = acts(i, 2 * (1 - x) + c)
-        return remote(s, s, ax_sem.at[i], ax_recv.at[i], across)
+        return remote(kept(0, i), kept(1, i), ax_sem.at[i], ax_recv.at[i], across)
 
     def acts_sib(i):
-        return remote(own_acts(i), acts(i, dp), as_sem.at[i], as_recv.at[i], sibling)
+        return remote(kept(0, i), acts(i, dp), as_sem.at[i], as_recv.at[i], sibling)
 
     def acts_from_sib(i):
         s = acts(i, 2 * x + 1 - c)
         return remote(s, s, as_sem.at[i], as_recv.at[i], sibling)
 
     def acts_on(i):
-        s = acts(i, 2 * (1 - x) + c)
-        return remote(s, s, as_sem.at[4 + i], as_recv.at[4 + i], sibling)
+        return remote(
+            kept(1, i), acts(i, 2 * (1 - x) + c), as_sem.at[4 + i], as_recv.at[4 + i], sibling)
 
     def acts_on_from(i):
         s = acts(i, 2 * (1 - x) + 1 - c)
         return remote(s, s, as_sem.at[4 + i], as_recv.at[4 + i], sibling)
 
-    def acts_local(i):
-        return pltpu.make_async_copy(own_acts(i), acts(i, dp), al_sem.at[i])
-
+    def acts_local(k, i):
+        index = dp if k == 0 else 2 * (1 - x) + c
+        return pltpu.make_async_copy(kept(k, i), acts(i, index), al_sem.at[4 * k + i])
+
+    def pass_acts(i):
+        acts_across(i).wait_recv()
+        acts_on(i).start()
+        acts_local(1, i).start()
+
+    held_load.wait()
     for i in range(4):
         acts_across(i).start()
     for i in range(4):
         acts_sib(i).start()
-        acts_local(i).start()
+        acts_local(0, i).start()
+
+    for i in range(5):
+        code_copy(i).start()
+
+    @pl.loop(0, depth // LANES)
+    def _(t):
+        r = pl.ds(pl.multiple_of(t * LANES, LANES), LANES)
+        scale[r, :] = jnp.broadcast_to(s_ref[r][None, :], (LANES, LANES)).T
 
     def relay_cross():
         for k in range(2):
@@ -197,6 +207,8 @@
             def _():
                 cross_down(k).start()
 
+    def side_cross():
+        for k in range(2):
             cross_side(k).start()
 
     def pass_side(d):
@@ -240,6 +252,7 @@
             pass_side(d - 2)
 
     g_local.wait()
+    pl.when(away < LINE - 1)(side_cross)
     for i in range(5):
         code_copy(i).wait()
 
@@ -253,9 +266,9 @@
         def _(t):
             r = pl.ds(pl.multiple_of(base + t * LANES, LANES), LANES)
             q = pl.ds(pl.multiple_of(t * LANES, LANES), LANES)
-            by = s_ref[r][None, :]
-            gs[:LANES, q] = (gbuf[0, r, :].astype(F32).T * by).astype(BF16)
-            gs[LANES:, q] = (gbuf[1, r, :].astype(F32).T * by).astype(BF16)
+            by = scale[r, :]
+            gs[q, :LANES] = (gbuf[0, r, :].astype(F32) * by).astype(BF16)
+            gs[q, LANES:] = (gbuf[1, r, :].astype(F32) * by).astype(BF16)
 
         tile = rows // 5
 
@@ -263,26 +276,32 @@
         def _(t):
             r = pl.ds(pl.multiple_of(t * tile, tile), tile)
             k = pl.ds(pl.multiple_of(base, LANES), half)
-            part = lax.dot_general(
-                gs[...], codes[r, k], (((1,), (1,)), ((), ())), preferred_element_type=F32)
-            acc[:, r] = part if first else acc[:, r] + part
+            part = jnp.dot(codes[r, k], gs[...], preferred_element_type=F32)
+            acc[r, :] = part if first else acc[r, :] + part
 
     near = lax.div(z, 2)
     multiply(near, True)
-    pl.when(away == LINE - 1)(relay_cross)
+
+    @pl.when(away == LINE - 1)
+    def _():
+        relay_cross()
+        side_cross()
+
     pass_side(LINE - 2)
     pass_side(LINE - 1)
     for i in range(2):
-        acts_from_across(i).wait_recv()
-        acts_on(i).start()
+        pass_acts(i)
     multiply(1 - near, False)
 
-    def tokens_of(core):
-        return pl.ds(pl.multiple_of(core * LANES, LANES), LANES)
+    @pl.loop(0, rows // LANES)
+    def _(t):
+        r = pl.ds(pl.multiple_of(t * LANES, LANES), LANES)
+        ig_sib[:, r] = acc[r, pl.ds(pl.multiple_of((1 - c) * LANES, LANES), LANES)].T
+        ig_own[:, r] = acc[r, pl.ds(pl.multiple_of(c * LANES, LANES), LANES)].T
 
     def ig_out():
         return remote(
-            acc.at[tokens_of(1 - c), pl.ds(pl.multiple_of(c * (rows - step_rows), LANES), step_rows)],
+            ig_sib.at[:, pl.ds(pl.multiple_of(c * (rows - step_rows), LANES), step_rows)],
             ig_ref.at[:, pl.ds(pl.multiple_of(c * rows, LANES), step_rows)],
             ig_sem.at[0], ig_sem.at[1], sibling)
 
@@ -291,13 +310,12 @@
         return remote(s, s, ig_sem.at[0], ig_sem.at[1], sibling)
 
     ig_local = pltpu.make_async_copy(
-        acc.at[tokens_of(c)], ig_ref.at[:, pl.ds(pl.multiple_of(c * step_rows, LANES), rows)], ig_sem.at[2])
+        ig_own, ig_ref.at[:, pl.ds(pl.multiple_of(c * step_rows, LANES), rows)], ig_sem.at[2])
     ig_out().start()
     ig_local.start()
 
     for i in range(2, 4):
-        acts_from_across(i).wait_recv()
-        acts_on(i).start()
+        pass_acts(i)
 
     block = pl.ds(pl.multiple_of(2 * entry * channels, 32), 2 * channels)
     og_copies = [
@@ -346,7 +364,8 @@
         acts_across(i).wait_send()
         acts_sib(i).wait_send()
         acts_on(i).wait_send()
-        acts_local(i).wait()
+        acts_local(0, i).wait()
+        acts_local(1, i).wait()
         acts_from_sib(i).wait_recv()
         acts_on_from(i).wait_recv()
     for copy in og_copies:
@@ -360,17 +379,18 @@
 PARTS = 4
 
 
-def weight_kernel(o_ref, a_ref, ig_ref, out_ref, ig_out, o, a, out, o_sem, a_sem, ig_sem, out_sem):
+def weight_kernel(o_ref, a_ref, ig_ref, out_ref, ig_out, o, a, out, ig, o_sem, a_sem, ig_sem, out_sem):
     channels = out_ref.shape[0]
     tokens = a_ref.shape[0] // 4
     loads = [pltpu.make_async_copy(o_ref.at[k], o.at[k], o_sem.at[k]) for k in range(4)]
     for k in range(4):
         rows = pl.ds(k * tokens, tokens)
         loads.append(pltpu.make_async_copy(a_ref.at[rows], a.at[rows], a_sem.at[k]))
-    ig_copy = pltpu.make_async_copy(ig_ref, ig_out, ig_sem.at[0])
+    ig_in = pltpu.make_async_copy(ig_ref, ig, ig_sem.at[0])
+    ig_copy = pltpu.make_async_copy(ig, ig_out, ig_sem.at[1])
     for load in loads:
         load.start()
-    ig_copy.start()
+    ig_in.start()
     for load in loads:
         load.wait()
 
@@ -401,6 +421,8 @@
         for i in range(PARTS):
             write(slot, t, i).start()
 
+    ig_in.wait()
+    ig_copy.start()
     last = full % 3
     for i in range(PARTS):
         write(last, full - 3, i).wait()
@@ -439,11 +461,15 @@
             pltpu.VMEM((rows, depth), BF16),
             pltpu.VMEM((2, depth, tokens), BF16),
             pltpu.VMEM((2, 2, channels, tokens), BF16),
-            pltpu.VMEM((2 * tokens, depth // 2), BF16),
-            pltpu.VMEM((2 * tokens, rows), F32),
+            pltpu.VMEM((depth // 2, 2 * tokens), BF16),
+            pltpu.VMEM((depth, LANES), F32),
+            pltpu.VMEM((rows, 2 * tokens), F32),
+            pltpu.VMEM((tokens, rows), F32),
+            pltpu.VMEM((tokens, rows), F32),
+            pltpu.VMEM((2, tokens, hidden), BF16),
             dma((5,)), dma((4,)), dma((4,)), dma((4,)), dma((8,)), dma((4,)), dma((4,)), dma((8,)),
             dma((1,)), dma((2,)), dma((2,)), dma((2,)), dma((2,)), dma((2,)),
-            dma((4,)), dma((8,)), dma((4,)), dma((8,)), dma((4,)), dma((6,)), dma((3,)), dma((1,)),
+            dma((4,)), dma((8,)), dma((4,)), dma((8,)), dma((8,)), dma((6,)), dma((3,)), dma((1,)), dma((1,)),
         ],
         compiler_params=pltpu.CompilerParams(
             collective_id=0, has_side_effects=True, vmem_limit_bytes=56 * 2**20),
@@ -460,7 +486,8 @@
             pltpu.VMEM((4, 2 * channels, tokens), BF16),
             pltpu.VMEM((4 * tokens, hidden), BF16),
             pltpu.VMEM((3, TILE, hidden), F32),
-            dma((4,)), dma((4,)), dma((1,)), dma((3, PARTS)),
+            pltpu.VMEM((tokens, hidden), F32),
+            dma((4,)), dma((4,)), dma((2,)), dma((3, PARTS)),
         ],
         compiler_params=pltpu.CompilerParams(vmem_limit_bytes=56 * 2**20),
     )(grads, acts, input_grads)

time: 119 us -> 68.3 us (0.57)
  Pallas kernels: 118 us -> 67.5 us
    pallas_call x1, Pallas kernels: 58.9 us -> 13.9 us  [per_device_kernels(): pl.pallas_call(weight_kernel, out_shape=(jax.ShapeDtypeStruct((2 * channe...]
    pallas_call x1, Pallas kernels: 59.1 us -> 53.6 us  [per_device_kernels(): pl.pallas_call(gather_kernel, out_shape=(jax.ShapeDtypeStruct((tokens, hi...]
where the time goes in v3:
time: 68.3 us; the launch traced here: 68.1 us
  Pallas kernels  67.5 us (99%)
    pallas_call x1, Pallas kernels, per_device_kernels(): pl.pallas_call(gather_kernel, out_shape=(jax.ShapeDtypeStruct((tokens, hi...  53.6 us
    pallas_call x1, Pallas kernels, per_device_kernels(): pl.pallas_call(weight_kernel, out_shape=(jax.ShapeDtypeStruct((2 * channe...  13.9 us

profile of v3, /device:TPU:7, one launch (start us, length us, event | category | flops | bytes accessed | tf_op | source)
XLA Modules:
  0.0 68.1 jit_solution(3984936622849043692)
XLA Ops:
  0.6 53.6 %shard_map.59 = (f32[128,3712]{1,0:T(8,128)}, bf16[512,3712]{1,0:T(8,128)(2,1)}, bf16[4,1856,128]{2,1,0:T(8,128)(2,1)}) custom-call(bf16[128,3712]{1,0:T(8,128)(2,1)} %a_ref.1, bf16[928,128]{1,0:T(8,128)(2,1)} %bitcast.2, f32[7424]{0:T(1024)} %s_ref.1, bf16[3712,7424]{1,0:T(8,128)(2,1)} %w_ref.1), custom_call_target="tpu_custom_call" | custom-call | tf_op jit(solution)/shard_map/pallas_call | solution.py:451
  54.2 13.9 %shard_map.60 = (f32[1856,3712]{1,0:T(8,128)}, f32[128,3712]{1,0:T(8,128)}) custom-call(bf16[4,1856,128]{2,1,0:T(8,128)(2,1)} %get-tuple-element.7.o_ref, bf16[512,3712]{1,0:T(8,128)(2,1)} %get-tuple-element.8.a_ref, f32[128,3712]{1,0:T(8,128)} %get-tuple-element.9.ig_ref), custom_call_target="tpu_custom_call" | custom-call | tf_op jit(solution)/shard_map/pallas_call | solution.py:477

commit v4 on v3

--- a/solution.py
+++ b/solution.py
@@ -28,7 +28,6 @@
     depth = w_ref.shape[1]
     rows = codes.shape[0]
     step_rows = hidden - rows
-    half = depth // 2
     sibling = (2 * x + 1 - c, j)
     across = (2 * (1 - x) + c, j)
     beside = (dp, 2 * z + 1 - y)
@@ -211,18 +210,46 @@
         for k in range(2):
             cross_side(k).start()
 
-    def pass_side(d):
-        def one(zz):
-            from_side(zz).wait_recv()
-            to_sib(zz, 1 - y).start()
-
-        if d == 0:
-            one(z)
-        else:
-            pl.when(z - d >= 0)(lambda: one(z - d))
-            pl.when(z + d <= LINE - 1)(lambda: one(z + d))
-
-    for d in range(1, LINE):
+    pair = 2 * channels
+    span = gs.shape[1]
+    tile = rows // 5
+
+    def multiply(zz, first, final):
+        for yy in range(2):
+            from_sib(zz, yy).wait_recv()
+        begin = pl.multiple_of(zz * pair, 64)
+        shift = pl.multiple_of((span - pair) * lax.rem(zz, 2), 64)
+        gs[zz, pl.ds(pl.multiple_of((1 - lax.rem(zz, 2)) * pair, 64), span - pair), :] = (
+            jnp.zeros((span - pair, 2 * LANES), BF16))
+
+        @pl.loop(0, pair // 64)
+        def _(t):
+            r = pl.ds(pl.multiple_of(begin + t * 64, 64), 64)
+            q = pl.ds(pl.multiple_of(shift + t * 64, 64), 64)
+            by = scale[r, :]
+            gs[zz, q, :LANES] = (gbuf[0, r, :].astype(F32) * by).astype(BF16)
+            gs[zz, q, LANES:] = (gbuf[1, r, :].astype(F32) * by).astype(BF16)
+
+        k = pl.ds(pl.multiple_of(lax.div(zz * pair, LANES) * LANES, LANES), span)
+
+        @pl.loop(0, 5)
+        def _(t):
+            if first:
+                code_copy(t).wait()
+            r = pl.ds(pl.multiple_of(t * tile, tile), tile)
+            part = jnp.dot(codes[r, k], gs[zz], preferred_element_type=F32)
+            if not first:
+                part = acc[r, :] + part
+            acc[r, :] = part
+            if final:
+                ig_sib[:, r] = acc[r, pl.ds(pl.multiple_of((1 - c) * LANES, LANES), LANES)].T
+                ig_own[:, r] = acc[r, pl.ds(pl.multiple_of(c * LANES, LANES), LANES)].T
+
+    def pass_side(zz):
+        from_side(zz).wait_recv()
+        to_sib(zz, 1 - y).start()
+
+    def relay(d):
         @pl.when(z - d >= 0)
         def _():
             zz = z - d
@@ -248,56 +275,34 @@
             to_sib(zz, y).start()
 
         pl.when(away == d - 1)(relay_cross)
-        if d >= 2:
-            pass_side(d - 2)
-
+
+    low = z < LINE // 2
+    end = jnp.logical_or(z == 0, z == LINE - 1)
+    second = jnp.where(z > 0, z - 1, 1)
+    third = jnp.where(end, jnp.where(low, 2, 1), z + 1)
+    fourth = jnp.where(low, LINE - 1, 0)
+
+    relay(1)
     g_local.wait()
+    pass_side(z)
+    multiply(z, True, False)
+    relay(2)
+    pass_side(second)
+    multiply(second, False, False)
+    relay(3)
     pl.when(away < LINE - 1)(side_cross)
-    for i in range(5):
-        code_copy(i).wait()
-
-    def multiply(h, first):
-        for zz in range(2):
-            for yy in range(2):
-                from_sib(2 * h + zz, yy).wait_recv()
-        base = h * half
-
-        @pl.loop(0, half // LANES)
-        def _(t):
-            r = pl.ds(pl.multiple_of(base + t * LANES, LANES), LANES)
-            q = pl.ds(pl.multiple_of(t * LANES, LANES), LANES)
-            by = scale[r, :]
-            gs[q, :LANES] = (gbuf[0, r, :].astype(F32) * by).astype(BF16)
-            gs[q, LANES:] = (gbuf[1, r, :].astype(F32) * by).astype(BF16)
-
-        tile = rows // 5
-
-        @pl.loop(0, 5)
-        def _(t):
-            r = pl.ds(pl.multiple_of(t * tile, tile), tile)
-            k = pl.ds(pl.multiple_of(base, LANES), half)
-            part = jnp.dot(codes[r, k], gs[...], preferred_element_type=F32)
-            acc[r, :] = part if first else acc[r, :] + part
-
-    near = lax.div(z, 2)
-    multiply(near, True)
+    pass_side(third)
+    multiply(third, False, False)
 
     @pl.when(away == LINE - 1)
     def _():
         relay_cross()
         side_cross()
 
-    pass_side(LINE - 2)
-    pass_side(LINE - 1)
     for i in range(2):
         pass_acts(i)
-    multiply(1 - near, False)
-
-    @pl.loop(0, rows // LANES)
-    def _(t):
-        r = pl.ds(pl.multiple_of(t * LANES, LANES), LANES)
-        ig_sib[:, r] = acc[r, pl.ds(pl.multiple_of((1 - c) * LANES, LANES), LANES)].T
-        ig_own[:, r] = acc[r, pl.ds(pl.multiple_of(c * LANES, LANES), LANES)].T
+    pass_side(fourth)
+    multiply(fourth, False, True)
 
     def ig_out():
         return remote(
@@ -375,38 +380,47 @@
     ig_in().wait_recv()
 
 
-TILE = 256
+WIDE = 512
 PARTS = 4
 
 
 def weight_kernel(o_ref, a_ref, ig_ref, out_ref, ig_out, o, a, out, ig, o_sem, a_sem, ig_sem, out_sem):
-    channels = out_ref.shape[0]
-    tokens = a_ref.shape[0] // 4
+    channels, hidden = out_ref.shape
+    full, rest = hidden // WIDE, hidden % WIDE
+    n = channels // PARTS
+
+    def load_a(t, width):
+        columns = pl.ds(pl.multiple_of(t * WIDE, LANES), width)
+        return pltpu.make_async_copy(a_ref.at[:, columns], a.at[:, columns], a_sem.at[t])
+
     loads = [pltpu.make_async_copy(o_ref.at[k], o.at[k], o_sem.at[k]) for k in range(4)]
-    for k in range(4):
-        rows = pl.ds(k * tokens, tokens)
-        loads.append(pltpu.make_async_copy(a_ref.at[rows], a.at[rows], a_sem.at[k]))
     ig_in = pltpu.make_async_copy(ig_ref, ig, ig_sem.at[0])
     ig_copy = pltpu.make_async_copy(ig, ig_out, ig_sem.at[1])
+    load_a(0, WIDE).start()
     for load in loads:
         load.start()
+    for t in range(1, full):
+        load_a(t, WIDE).start()
+    load_a(full, rest).start()
     ig_in.start()
     for load in loads:
         load.wait()
 
-    full = channels // TILE
-    rest = channels % TILE
-    n = TILE // PARTS
-
-    def write(slot, t, i):
-        start = pl.multiple_of(t * TILE + i * n, n)
+    def write(slot, t, i, width=WIDE):
+        rows = pl.ds(pl.multiple_of(i * n, 16), n)
         return pltpu.make_async_copy(
-            out.at[slot, pl.ds(i * n, n)], out_ref.at[pl.ds(start, n)], out_sem.at[slot, i])
-
-    def product(start, size):
-        rows = pl.ds(start, size)
-        left = jnp.concatenate([o[k, rows, :] for k in range(4)], axis=1)
-        return jnp.dot(left, a[...], preferred_element_type=F32)
+            out.at[slot, rows, pl.ds(0, width)],
+            out_ref.at[rows, pl.ds(pl.multiple_of(t * WIDE, LANES), width)], out_sem.at[slot, i])
+
+    def work(slot, t, width):
+        columns = pl.ds(pl.multiple_of(t * WIDE, LANES), width)
+
+        @pl.loop(0, PARTS)
+        def _(i):
+            rows = pl.ds(pl.multiple_of(i * n, 16), n)
+            left = jnp.concatenate([o[k, rows, :] for k in range(4)], axis=1)
+            out[slot, rows, :width] = jnp.dot(left, a[:, columns], preferred_element_type=F32)
+            write(slot, t, i, width).start()
 
     @pl.loop(0, full)
     def _(t):
@@ -417,26 +431,21 @@
             for i in range(PARTS):
                 write(slot, t - 3, i).wait()
 
-        out[slot] = product(pl.multiple_of(t * TILE, TILE), TILE)
-        for i in range(PARTS):
-            write(slot, t, i).start()
+        load_a(t, WIDE).wait()
+        work(slot, t, WIDE)
 
     ig_in.wait()
     ig_copy.start()
     last = full % 3
     for i in range(PARTS):
         write(last, full - 3, i).wait()
-    out[last, :rest] = product(full * TILE, rest)
-    ends = []
-    for i in range(rest // n):
-        ends.append(write(last, full, i))
-    for end in ends:
-        end.start()
+    load_a(full, rest).wait()
+    work(last, full, rest)
     for t in (full - 2, full - 1):
         for i in range(PARTS):
             write(t % 3, t, i).wait()
-    for end in ends:
-        end.wait()
+    for i in range(PARTS):
+        write(last, full, i, rest).wait()
     ig_copy.wait()
 
 
@@ -461,7 +470,7 @@
             pltpu.VMEM((rows, depth), BF16),
             pltpu.VMEM((2, depth, tokens), BF16),
             pltpu.VMEM((2, 2, channels, tokens), BF16),
-            pltpu.VMEM((depth // 2, 2 * tokens), BF16),
+            pltpu.VMEM((LINE, pl.cdiv(2 * channels, LANES) * LANES, 2 * tokens), BF16),
             pltpu.VMEM((depth, LANES), F32),
             pltpu.VMEM((rows, 2 * tokens), F32),
             pltpu.VMEM((tokens, rows), F32),
@@ -485,9 +494,9 @@
         scratch_shapes=[
             pltpu.VMEM((4, 2 * channels, tokens), BF16),
             pltpu.VMEM((4 * tokens, hidden), BF16),
-            pltpu.VMEM((3, TILE, hidden), F32),
+            pltpu.VMEM((3, 2 * channels, WIDE), F32),
             pltpu.VMEM((tokens, hidden), F32),
-            dma((4,)), dma((4,)), dma((2,)), dma((3, PARTS)),
+            dma((4,)), dma((hidden // WIDE + 1,)), dma((2,)), dma((3, PARTS)),
         ],
         compiler_params=pltpu.CompilerParams(vmem_limit_bytes=56 * 2**20),
     )(grads, acts, input_grads)

time: 68.3 us -> 65.5 us (0.959)
  Pallas kernels: 67.5 us -> 64.1 us
    pallas_call x1, Pallas kernels: 53.6 us -> 47.8 us  [per_device_kernels(): pl.pallas_call(gather_kernel, out_shape=(jax.ShapeDtypeStruct((tokens, hi...]
    pallas_call x1, Pallas kernels: 13.9 us -> 16.3 us  [per_device_kernels(): pl.pallas_call(weight_kernel, out_shape=(jax.ShapeDtypeStruct((2 * channe...]
where the time goes in v4:
time: 65.5 us; the launch traced here: 64.7 us
  Pallas kernels  64.1 us (98%)
    pallas_call x1, Pallas kernels, per_device_kernels(): pl.pallas_call(gather_kernel, out_shape=(jax.ShapeDtypeStruct((tokens, hi...  47.8 us
    pallas_call x1, Pallas kernels, per_device_kernels(): pl.pallas_call(weight_kernel, out_shape=(jax.ShapeDtypeStruct((2 * channe...  16.3 us

profile of v4, /device:TPU:7, one launch (start us, length us, event | category | flops | bytes accessed | tf_op | source)
XLA Modules:
  0.0 64.7 jit_solution(1295658020963358207)
XLA Ops:
  0.6 47.8 %shard_map.59 = (f32[128,3712]{1,0:T(8,128)}, bf16[512,3712]{1,0:T(8,128)(2,1)}, bf16[4,1856,128]{2,1,0:T(8,128)(2,1)}) custom-call(bf16[128,3712]{1,0:T(8,128)(2,1)} %a_ref.1, bf16[928,128]{1,0:T(8,128)(2,1)} %bitcast.2, f32[7424]{0:T(1024)} %s_ref.1, bf16[3712,7424]{1,0:T(8,128)(2,1)} %w_ref.1), custom_call_target="tpu_custom_call" | custom-call | tf_op jit(solution)/shard_map/pallas_call | solution.py:460
  48.4 16.3 %shard_map.60 = (f32[1856,3712]{1,0:T(8,128)}, f32[128,3712]{1,0:T(8,128)}) custom-call(bf16[4,1856,128]{2,1,0:T(8,128)(2,1)} %get-tuple-element.7.o_ref, bf16[512,3712]{1,0:T(8,128)(2,1)} %get-tuple-element.8.a_ref, f32[128,3712]{1,0:T(8,128)} %get-tuple-element.9.ig_ref), custom_call_target="tpu_custom_call" | custom-call | tf_op jit(solution)/shard_map/pallas_call | solution.py:486

commit v5 on v4

--- a/solution.py
+++ b/solution.py
@@ -18,7 +18,7 @@
     codes, gbuf, cross, gs, scale, acc, ig_own, ig_sib, held,
     code_sem, up_sem, down_sem, y_sem, sib_sem, line_recv, y_recv, sib_recv,
     cross_sem, cup_sem, cdown_sem, cy_sem, cross_recv, cy_recv,
-    ax_sem, as_sem, ax_recv, as_recv, al_sem, og_sem, ig_sem, g_sem, held_sem,
+    ax_sem, as_sem, ax_recv, as_recv, al_sem, og_sem, ig_sem, g_sem, held_sem, far_sem,
 ):
     dp, j = lax.axis_index("dp"), lax.axis_index("tensor")
     x, c = lax.div(dp, 2), lax.rem(dp, 2)
@@ -294,14 +294,20 @@
     pass_side(third)
     multiply(third, False, False)
 
-    @pl.when(away == LINE - 1)
-    def _():
-        relay_cross()
-        side_cross()
-
     for i in range(2):
         pass_acts(i)
     pass_side(fourth)
+
+    sends_far = jnp.logical_and(end, jnp.logical_not(sends_cross))
+
+    def far_out():
+        return remote(slot(c, fourth, 1 - y), cross.at[c, 1 - y], far_sem.at[0], cy_recv.at[c],
+                      (2 * (1 - x) + lax.rem(fourth, 2), j))
+
+    @pl.when(sends_far)
+    def _():
+        far_out().start()
+
     multiply(fourth, False, True)
 
     def ig_out():
@@ -321,6 +327,8 @@
 
     for i in range(2, 4):
         pass_acts(i)
+
+    pl.when(away == LINE - 1)(relay_cross)
 
     block = pl.ds(pl.multiple_of(2 * entry * channels, 32), 2 * channels)
     og_copies = [
@@ -363,7 +371,13 @@
         def _():
             cross_down(k).wait_send()
 
-        cross_side(k).wait_send()
+        @pl.when(away < LINE - 1)
+        def _():
+            cross_side(k).wait_send()
+
+    @pl.when(sends_far)
+    def _():
+        far_out().wait_send()
 
     for i in range(4):
         acts_across(i).wait_send()
@@ -380,47 +394,38 @@
     ig_in().wait_recv()
 
 
-WIDE = 512
+TILE = 256
 PARTS = 4
 
 
 def weight_kernel(o_ref, a_ref, ig_ref, out_ref, ig_out, o, a, out, ig, o_sem, a_sem, ig_sem, out_sem):
-    channels, hidden = out_ref.shape
-    full, rest = hidden // WIDE, hidden % WIDE
-    n = channels // PARTS
-
-    def load_a(t, width):
-        columns = pl.ds(pl.multiple_of(t * WIDE, LANES), width)
-        return pltpu.make_async_copy(a_ref.at[:, columns], a.at[:, columns], a_sem.at[t])
-
+    channels = out_ref.shape[0]
+    tokens = a_ref.shape[0] // 4
     loads = [pltpu.make_async_copy(o_ref.at[k], o.at[k], o_sem.at[k]) for k in range(4)]
+    for k in range(4):
+        rows = pl.ds(k * tokens, tokens)
+        loads.append(pltpu.make_async_copy(a_ref.at[rows], a.at[rows], a_sem.at[k]))
     ig_in = pltpu.make_async_copy(ig_ref, ig, ig_sem.at[0])
     ig_copy = pltpu.make_async_copy(ig, ig_out, ig_sem.at[1])
-    load_a(0, WIDE).start()
     for load in loads:
         load.start()
-    for t in range(1, full):
-        load_a(t, WIDE).start()
-    load_a(full, rest).start()
     ig_in.start()
     for load in loads:
         load.wait()
 
-    def write(slot, t, i, width=WIDE):
-        rows = pl.ds(pl.multiple_of(i * n, 16), n)
+    full = channels // TILE
+    rest = channels % TILE
+    n = TILE // PARTS
+
+    def write(slot, t, i):
+        start = pl.multiple_of(t * TILE + i * n, n)
         return pltpu.make_async_copy(
-            out.at[slot, rows, pl.ds(0, width)],
-            out_ref.at[rows, pl.ds(pl.multiple_of(t * WIDE, LANES), width)], out_sem.at[slot, i])
-
-    def work(slot, t, width):
-        columns = pl.ds(pl.multiple_of(t * WIDE, LANES), width)
-
-        @pl.loop(0, PARTS)
-        def _(i):
-            rows = pl.ds(pl.multiple_of(i * n, 16), n)
-            left = jnp.concatenate([o[k, rows, :] for k in range(4)], axis=1)
-            out[slot, rows, :width] = jnp.dot(left, a[:, columns], preferred_element_type=F32)
-            write(slot, t, i, width).start()
+            out.at[slot, pl.ds(i * n, n)], out_ref.at[pl.ds(start, n)], out_sem.at[slot, i])
+
+    def product(start, size):
+        rows = pl.ds(start, size)
+        left = jnp.concatenate([o[k, rows, :] for k in range(4)], axis=1)
+        return jnp.dot(left, a[...], preferred_element_type=F32)
 
     @pl.loop(0, full)
     def _(t):
@@ -431,21 +436,26 @@
             for i in range(PARTS):
                 write(slot, t - 3, i).wait()
 
-        load_a(t, WIDE).wait()
-        work(slot, t, WIDE)
+        out[slot] = product(pl.multiple_of(t * TILE, TILE), TILE)
+        for i in range(PARTS):
+            write(slot, t, i).start()
 
     ig_in.wait()
     ig_copy.start()
     last = full % 3
     for i in range(PARTS):
         write(last, full - 3, i).wait()
-    load_a(full, rest).wait()
-    work(last, full, rest)
+    out[last, :rest] = product(full * TILE, rest)
+    ends = []
+    for i in range(rest // n):
+        ends.append(write(last, full, i))
+    for end in ends:
+        end.start()
     for t in (full - 2, full - 1):
         for i in range(PARTS):
             write(t % 3, t, i).wait()
-    for i in range(PARTS):
-        write(last, full, i, rest).wait()
+    for end in ends:
+        end.wait()
     ig_copy.wait()
 
 
@@ -478,7 +488,7 @@
             pltpu.VMEM((2, tokens, hidden), BF16),
             dma((5,)), dma((4,)), dma((4,)), dma((4,)), dma((8,)), dma((4,)), dma((4,)), dma((8,)),
             dma((1,)), dma((2,)), dma((2,)), dma((2,)), dma((2,)), dma((2,)),
-            dma((4,)), dma((8,)), dma((4,)), dma((8,)), dma((8,)), dma((6,)), dma((3,)), dma((1,)), dma((1,)),
+            dma((4,)), dma((8,)), dma((4,)), dma((8,)), dma((8,)), dma((6,)), dma((3,)), dma((1,)), dma((1,)), dma((1,)),
         ],
         compiler_params=pltpu.CompilerParams(
             collective_id=0, has_side_effects=True, vmem_limit_bytes=56 * 2**20),
@@ -494,9 +504,9 @@
         scratch_shapes=[
             pltpu.VMEM((4, 2 * channels, tokens), BF16),
             pltpu.VMEM((4 * tokens, hidden), BF16),
-            pltpu.VMEM((3, 2 * channels, WIDE), F32),
+            pltpu.VMEM((3, TILE, hidden), F32),
             pltpu.VMEM((tokens, hidden), F32),
-            dma((4,)), dma((hidden // WIDE + 1,)), dma((2,)), dma((3, PARTS)),
+            dma((4,)), dma((4,)), dma((2,)), dma((3, PARTS)),
         ],
         compiler_params=pltpu.CompilerParams(vmem_limit_bytes=56 * 2**20),
     )(grads, acts, input_grads)

time: 65.5 us -> 63 us (0.962)
  the two profiles are of different devices: /device:TPU:7 before, /device:TPU:0 now
where the time goes in v5:
time: 63 us; the launch traced here: 62.8 us
  Pallas kernels  62.2 us (99%)
  between operations  0.64 us (1%)
    pallas_call x1, Pallas kernels, per_device_kernels(): pl.pallas_call(gather_kernel, out_shape=(jax.ShapeDtypeStruct((tokens, hi...  48.3 us
    pallas_call x1, Pallas kernels, per_device_kernels(): pl.pallas_call(weight_kernel, out_shape=(jax.ShapeDtypeStruct((2 * channe...  13.9 us

profile of v5, /device:TPU:0, one launch (start us, length us, event | category | flops | bytes accessed | tf_op | source)
XLA Modules:
  0.0 62.8 jit_solution(16705889027526959942)
XLA Ops:
  0.6 48.3 %shard_map.59 = (f32[128,3712]{1,0:T(8,128)}, bf16[512,3712]{1,0:T(8,128)(2,1)}, bf16[4,1856,128]{2,1,0:T(8,128)(2,1)}) custom-call(bf16[128,3712]{1,0:T(8,128)(2,1)} %a_ref.1, bf16[928,128]{1,0:T(8,128)(2,1)} %bitcast.2, f32[7424]{0:T(1024)} %s_ref.1, bf16[3712,7424]{1,0:T(8,128)(2,1)} %w_ref.1), custom_call_target="tpu_custom_call" | custom-call | tf_op jit(solution)/shard_map/pallas_call | solution.py:470
  49.0 13.9 %shard_map.60 = (f32[1856,3712]{1,0:T(8,128)}, f32[128,3712]{1,0:T(8,128)}) custom-call(bf16[4,1856,128]{2,1,0:T(8,128)(2,1)} %get-tuple-element.7.o_ref, bf16[512,3712]{1,0:T(8,128)(2,1)} %get-tuple-element.8.a_ref, f32[128,3712]{1,0:T(8,128)} %get-tuple-element.9.ig_ref), custom_call_target="tpu_custom_call" | custom-call | tf_op jit(solution)/shard_map/pallas_call | solution.py:496
